TPU v7x, 32 devices: a whole 2x2x4 slice. The times are simulated.
32 devices in a mesh: group: 2 (over x), prow: 8 (over z, y), pcol: 2 (over core).
Axes of the slice: x: 2, y: 2, z: 4, core: 2. Of those that a mesh axis runs over, the one named last changes fastest.
Arguments:
- orbitals: bfloat16 [32768, 1024], P(('group', 'prow', 'pcol')), parts along dimension 0, may hold values from -6 to 6
- points: int32 [4096], P(('group', 'prow', 'pcol')), parts along dimension 0, may hold values from 0 to 1023, as said below
- kernel: bfloat16 [4096, 8, 2, 128], P(('group', 'prow'), None, 'pcol'), parts along dimension 0, may hold values from -0.009765625 to 0.009765625
Outputs:
- exchange: bfloat16 [4096, 1024], P(('group', 'prow'), 'pcol'), parts along dimension 0
There are 2 independent parts, one for each index of `group`. A program takes and returns all parts, laid end to end along the dimension named above; each array names one. Nothing has to cross between parts.
Inputs may be any that keep to these rules, and one draw needn't show every extreme that they name: Within one block of 128 consecutive points the values are distinct; value v in block b names grid row b * 1024 + v.
All inputs are finite; a program needn't handle non-finite values.
Results may differ from a plain program's by a relative error of at most 0.0051.
Values may be sent and summed in bfloat16 or wider, within the bound.
A program may use at most 128 MiB of HBM per device.

v0:
```python
import jax
import jax.numpy as jnp
from jax import lax
from jax.sharding import PartitionSpec as P


def gram_rows(left_rows, right_rows):
    return lax.dot_general(
        left_rows, right_rows, (((1,), (1,)), ((), ())), preferred_element_type=jnp.float32
    )


def shards(orbitals, points, kernel):
    sampled = jnp.take(orbitals, points, axis=0)
    own_rows = lax.all_gather(sampled, "pcol", axis=0, tiled=True)
    row_total = own_rows.shape[0]
    kernel_tile = kernel.reshape(row_total, -1)
    column_values = lax.all_gather(sampled, "prow", axis=0, tiled=True)
    density = gram_rows(own_rows, column_values)
    screened = (kernel_tile * density).astype(jnp.bfloat16)
    partial_sum = jnp.dot(screened, column_values, preferred_element_type=jnp.float32)
    result = lax.psum_scatter(partial_sum, "pcol", scatter_dimension=1, tiled=True).astype(
        jnp.bfloat16
    )
    return result


def solution(mesh):
    in_specs = (
        P(("group", "prow", "pcol"), None),
        P(("group", "prow", "pcol")),
        P(("group", "prow"), None, "pcol", None),
    )
    out_specs = P(("group", "prow"), "pcol")
    return jax.shard_map(shards, mesh=mesh, in_specs=in_specs, out_specs=out_specs, check_vma=False)
```

profile of v0, /device:TPU:1, one launch (start us, length us, event | category | flops | bytes accessed | tf_op | source)
XLA Modules:
  0.0 82.3 jit_solution(11710175654006554776)
XLA Ops:
  6.5 0.0 copy-start
  6.5 0.0 all-gather.2.cloned.1.call-start
  6.5 0.8 compare_and_fusion
  7.4 0.7 compare_select_fusion
  8.0 0.1 copy-done
  8.1 0.9 %gather_fusion = bf16[128,1024]{1,0:T(8,128)(2,1)S(1)} fusion(bf16[1024,1024]{1,0:T(8,128)(2,1)S(1)} %copy-done, s32[1024]{0:T(1024)S(1)} %pad_clamp_fusion), kind=kCustom, calls=%fused_computation | custom fusion | bytes 524800 | tf_op jit(solution)/shard_map/jit(_take)/gather | solution.py:14
  9.0 0.8 broadcast_select_fusion
  9.8 0.0 all-gather.2.cloned.1.call-update
  9.8 0.0 reduce-scatter.2.cloned.1.call-start
  9.9 1.1 %convert.2 = f32[32,8,8,128]{3,2,1,0:T(8,128)S(1)} convert(bf16[32,8,8,128]{3,2,1,0:T(8,128)(2,1)} %bitcast.12) | non-fusion elementwise | flops 262144 | bytes 1572864
  11.0 3.8 %all_gather.6 = bf16[256,1024]{1,0:T(8,128)(2,1)} all-gather(bf16[128,1024]{1,0:T(8,128)(2,1)} %broadcast_select_fusion), channel_id=1, replica_groups=mesh['group'=2,'prow'=8,'pcol'=2] {'pcol'}, dimensions={0}, use_global_device_ids=true | all-gather | bytes 786432 | tf_op jit(solution)/shard_map/all_gather | solution.py:15
  14.9 45.4 %all-gather.2.cloned.1.call-done = bf16[1024,1024]{1,0:T(8,128)(2,1)} async-done(((bf16[128,1024]{1,0:T(8,128)(2,1)}), bf16[1024,1024]{1,0:T(8,128)(2,1)}) %all-gather.2.cloned.1.call-update) | async-done | bytes 2097168 | tf_op jit(solution)/shard_map/all_gather | solution.py:18
  60.2 4.8 %fusion.1 = f32[256,1024]{1,0:T(8,128)} fusion(bf16[1024,1024]{1,0:T(8,128)(2,1)} %all-gather.2.cloned.1.call-done, bf16[256,1024]{1,0:T(8,128)(2,1)} %all_gather.6, f32[32,8,8,128]{3,2,1,0:T(8,128)S(1)} %convert.2), kind=kOutput, calls=%fused_computation.3 | convolution fusion | flops 1074266112 | bytes 4718592 | tf_op jit(solution)/shard_map/dot_general | solution.py:21
  65.0 0.0 reduce-scatter.2.cloned.1.call-update
  65.0 8.7 %reduce-scatter.2.cloned.1.call-done = f32[256,512]{1,0:T(8,128)} async-done(((f32[256,1024]{1,0:T(8,128)}), f32[256,512]{1,0:T(8,128)}) %reduce-scatter.2.cloned.1.call-update) | async-done | bytes 524304 | tf_op jit(solution)/shard_map/reduce_scatter | solution.py:22
  73.7 1.8 %convert_element_type.15 = bf16[256,512]{1,0:T(8,128)(2,1)} convert(f32[256,512]{1,0:T(8,128)} %reduce-scatter.2.cloned.1.call-done) | non-fusion elementwise | flops 131072 | bytes 786432 | tf_op jit(solution)/shard_map/convert_element_type | solution.py:22
  (1 shorter events, 0.0 us)
Async XLA Ops:
  6.5 1.6 %copy-start = (bf16[1024,1024]{1,0:T(8,128)(2,1)S(1)}, bf16[1024,1024]{1,0:T(8,128)(2,1)}, u32[]{:S(2)}) copy-start(bf16[1024,1024]{1,0:T(8,128)(2,1)} %param.3) | copy-start | bytes 6291460
  6.5 53.7 %all-gather.2.cloned.1.call-start = ((), (), s32[]{:S(2)}) async-start(), calls=%async_computation.1 | async-start | bytes 2359296 | tf_op jit(solution)/shard_map/all_gather | solution.py:18
  9.8 63.9 %reduce-scatter.2.cloned.1.call-start = ((), (), s32[]{:S(2)}) async-start(), calls=%async_computation.2 | async-start | bytes 1572864 | tf_op jit(solution)/shard_map/reduce_scatter | solution.py:22
Sparse Core Ops, SparseCore 0:
  9.9 50.2 all-gather.1
  65.2 8.4 reduce-scatter.1
where the time goes:
time: 82.9 us; the launch traced here: 82.3 us
  waiting for transfers between devices  54.1 us (65%)
  between operations  13.4 us (16%)
  other arithmetic  5.2 us (6%)
  matrix products  4.77 us (6%)
  blocking collectives  3.82 us (5%)
  local copies, waits for them, and re-layouts  0.99 us (1%)
    all_gather x1, waiting for transfers between devices, shards(): column_values = lax.all_gather(sampled, 'prow', axis=0, tiled=True)  45.4 us
    reduce_scatter x1, waiting for transfers between devices, shards(): lax.psum_scatter(partial_sum, 'pcol', scatter_dimension=1, tiled=True)  8.66 us
    dot_general x1, matrix products, shards(): jnp.dot(screened, column_values, preferred_element_type=jnp.float32)  4.77 us
    all_gather x1, blocking collectives, shards(): own_rows = lax.all_gather(sampled, 'pcol', axis=0, tiled=True)  3.82 us
    convert_element_type x1, other arithmetic, shards(): lax.psum_scatter(partial_sum, 'pcol', scatter_dimension=1, tiled=True)  1.77 us
  transfers between devices with their start and end apart: 2, of which 2 were waited for; matrix products, arithmetic and copies ran while one was open for 1% of the time, Pallas kernels for 0%

commit v1 on v0

v1 whole, which is shorter than its diff:
```python
import functools

import jax
import jax.numpy as jnp
from jax import lax
from jax.experimental import pallas as pl
from jax.experimental.pallas import tpu as pltpu
from jax.sharding import PartitionSpec as P

MESH = pl.DeviceIdType.MESH
CH = 4
HALF = CH // 2


def ring_index(pos, n):
    return jnp.where(pos < n // 2, 2 * pos, 2 * (n - 1 - pos) + 1)


def dot(a, b):
    return jnp.dot(a, b, preferred_element_type=jnp.float32)


def dot_t(a, b):
    return lax.dot_general(a, b, (((1,), (1,)), ((), ())), preferred_element_type=jnp.float32)


def body(
    n, orb_hbm, pts_ref, ker_hbm, out_ref,
    orb, ker, ker32, rows, blocks, sib_blocks, scr, sib_scr, acc,
    orb_sem, ker_sem, row_send, row_recv, ring_send, ring_recv, blk_send, blk_recv, scr_send, scr_recv,
):
    last = n // 2
    pts = pts_ref.shape[1]
    grid_rows, wide = orb.shape[1], orb.shape[2]
    group, prow, core = lax.axis_index("group"), lax.axis_index("prow"), lax.axis_index("pcol")
    pos = jnp.where(prow % 2 == 0, prow // 2, n - 1 - prow // 2)
    right = (group, ring_index((pos + 1) % n, n), core)
    left = (group, ring_index((pos + n - 1) % n, n), core)
    sibling = (group, prow, 1 - core)
    mine = pl.ds(pl.multiple_of(core * pts, pts), pts)
    theirs = pl.ds(pl.multiple_of((1 - core) * pts, pts), pts)
    side = (pl.ds(0, pts), pl.ds(pts, pts))

    def remote(src, dst, send, recv, device):
        return pltpu.make_async_remote_copy(
            src_ref=src, dst_ref=dst, send_sem=send, recv_sem=recv, device_id=device, device_id_type=MESH
        )

    def hop(way, s, c):
        static_first = isinstance(s, int) and s == 0
        static_last = isinstance(s, int) and s == last - 1
        src = rows.at[c, mine] if static_first else blocks.at[s, c, side[way]]
        dst = blocks.at[s + 1, c, side[0] if static_last else side[way]]
        return remote(
            src, dst, ring_send.at[way, s, c], ring_recv.at[way, s + 1, c], right if way == 0 else left
        )

    def row_copy(c):
        return remote(rows.at[c, mine], rows.at[c, mine], row_send.at[c], row_recv.at[c], sibling)

    def row_arrival(c):
        return remote(rows.at[c, theirs], rows.at[c, theirs], row_send.at[c], row_recv.at[c], sibling)

    def blk_copy(s, at_last=False):
        far = pl.ds((1 - core) * HALF, HALF)
        if at_last:
            return remote(
                blocks.at[s, far, side[0]], sib_blocks.at[s, :, side[0]], blk_send.at[s], blk_recv.at[s], sibling
            )
        return remote(blocks.at[s, far], sib_blocks.at[s], blk_send.at[s], blk_recv.at[s], sibling)

    def scr_copy(s, narrow=False):
        if narrow:
            return remote(
                scr.at[s, :, side[0]], sib_scr.at[s, :, side[0]], scr_send.at[s], scr_recv.at[s], sibling
            )
        return remote(scr.at[s], sib_scr.at[s], scr_send.at[s], scr_recv.at[s], sibling)

    def kernel_columns(index):
        return ker32[pl.ds(index, out_ref.shape[0], stride=n), :]

    order = (0, 2, 1, 3)
    loads = [
        pltpu.make_async_copy(orb_hbm.at[:, pl.ds(c * wide, wide)], orb.at[c], orb_sem.at[c]) for c in range(CH)
    ]
    for c in order:
        loads[c].start()
    ker_load = pltpu.make_async_copy(ker_hbm, ker, ker_sem)
    ker_load.start()

    barrier = pltpu.get_barrier_semaphore()
    for device in (left, right, sibling):
        pl.semaphore_signal(barrier, inc=1, device_id=device, device_id_type=MESH)

    wanted = jnp.transpose(jnp.broadcast_to(pts_ref[...], (pts, pts)))
    wanted = jnp.concatenate([wanted] * (grid_rows // pts), axis=1)
    hot = (wanted == lax.broadcasted_iota(jnp.int32, (pts, grid_rows), 1)).astype(jnp.float32).astype(jnp.bfloat16)

    for k, c in enumerate(order):
        loads[c].wait()
        rows[c, mine] = dot(hot, orb[c]).astype(jnp.bfloat16)
        if k == 0:
            pl.semaphore_wait(barrier, 3)
        hop(0 if c < HALF else 1, 0, c).start()
        row_copy(c).start()
    for c in range(HALF):
        hop(0, 0, c + HALF).start()
        hop(1, 0, c).start()

    ker_load.wait()
    ker32[...] = ker[...].astype(jnp.float32).reshape(ker32.shape)

    for c in range(CH):
        row_arrival(c).wait_recv()
    density = dot_t(rows[0], rows[0, mine])
    for c in range(1, CH):
        density += dot_t(rows[c], rows[c, mine])
    screened = (kernel_columns(prow) * density).astype(jnp.bfloat16)
    scr[0, :, side[0]] = screened
    scr_copy(0, True).start()
    for i in range(HALF):
        acc[i] = dot(screened, rows[core * HALF + i, mine])

    def late(s):
        scr_copy(s).wait_recv()
        blk_copy(s).wait_recv()
        for i in range(HALF):
            acc[i] += dot(sib_scr[s], sib_blocks[s, i])

    def late_first():
        scr_copy(0, True).wait_recv()
        for i in range(HALF):
            acc[i] += dot(sib_scr[0, :, side[0]], rows[core * HALF + i, theirs])

    def step(s):
        for k in range(CH):
            for way in (0, 1):
                c = (k + way * HALF) % CH
                hop(way, s - 1, c).wait_recv()
                if not isinstance(s, int) or s < last - 1 or k < HALF:
                    hop(way, s, c).start()
        blk_copy(s).start()
        density = dot_t(rows[0], blocks[s, 0])
        for c in range(1, CH):
            density += dot_t(rows[c], blocks[s, c])
        from_left = kernel_columns(ring_index((pos + n - s) % n, n))
        from_right = kernel_columns(ring_index((pos + s) % n, n))
        screened = (jnp.concatenate([from_left, from_right], axis=1) * density).astype(jnp.bfloat16)
        scr[s] = screened
        scr_copy(s).start()
        for i in range(HALF):
            acc[i] += dot(screened, blocks[s, core * HALF + i])

    step(1)
    late_first()

    if last == 4:
        step(2)
        late(1)
    else:

        @pl.loop(2, last - 1)
        def _(s):
            step(s)
            late(s - 1)

    step(last - 1)
    late(last - 2)

    far = side[0]
    for k in range(HALF):
        hop(0, last - 1, k).wait_recv()
        hop(1, last - 1, k + HALF).wait_recv()
        part = dot_t(rows[k], blocks[last, k, far]) + dot_t(rows[k + HALF], blocks[last, k + HALF, far])
        density = part if k == 0 else density + part
    blk_copy(last, True).start()
    screened = (kernel_columns(ring_index((pos + last) % n, n)) * density).astype(jnp.bfloat16)
    scr[last, :, far] = screened
    scr_copy(last, True).start()
    late(last - 1)
    for i in range(HALF):
        acc[i] += dot(screened, blocks[last, core * HALF + i, far])
    blk_copy(last, True).wait_recv()
    scr_copy(last, True).wait_recv()
    for i in range(HALF):
        total = acc[i] + dot(sib_scr[last, :, far], sib_blocks[last, i, far])
        out_ref[:, pl.ds(i * wide, wide)] = total.astype(out_ref.dtype)

    for c in range(CH):
        row_copy(c).wait_send()
        for way in (0, 1):
            hop(way, 0, c).wait_send()
            hop(way, 1, c).wait_send()

    def drain(s):
        for c in range(CH):
            for way in (0, 1):
                hop(way, s, c).wait_send()

    if last == 4:
        drain(2)
    else:
        pl.loop(2, last - 1)(drain)
    for k in range(HALF):
        hop(0, last - 1, k).wait_send()
        hop(1, last - 1, k + HALF).wait_send()
    scr_copy(0, True).wait_send()
    scr_copy(last, True).wait_send()
    blk_copy(last, True).wait_send()

    def drain_pair(s):
        scr_copy(s).wait_send()
        blk_copy(s).wait_send()

    if last == 4:
        for s in range(1, last):
            drain_pair(s)
    else:
        pl.loop(1, last)(drain_pair)


def shards(n, orbitals, points, kernel):
    grid_rows, nocc = orbitals.shape
    pts = points.shape[0]
    row_total = kernel.shape[0]
    wide = nocc // CH
    slots = n // 2 + 1
    bf16, f32 = jnp.bfloat16, jnp.float32
    dma = pltpu.SemaphoreType.DMA
    scratch = [
        pltpu.VMEM((CH, grid_rows, wide), bf16),
        pltpu.VMEM((row_total, n, pts), bf16),
        pltpu.VMEM((row_total * n, pts), f32),
        pltpu.VMEM((CH, row_total, wide), bf16),
        pltpu.VMEM((slots, CH, 2 * pts, wide), bf16),
        pltpu.VMEM((slots, HALF, 2 * pts, wide), bf16),
        pltpu.VMEM((slots, row_total, 2 * pts), bf16),
        pltpu.VMEM((slots, row_total, 2 * pts), bf16),
        pltpu.VMEM((HALF, row_total, wide), f32),
        dma((CH,)),
        dma,
        dma((CH,)),
        dma((CH,)),
        dma((2, slots, CH)),
        dma((2, slots, CH)),
        dma((slots,)),
        dma((slots,)),
        dma((slots,)),
        dma((slots,)),
    ]
    flops = 4 * row_total * n * pts * nocc
    return pl.pallas_call(
        functools.partial(body, n),
        out_shape=jax.ShapeDtypeStruct((row_total, nocc // 2), bf16),
        in_specs=[
            pl.BlockSpec(memory_space=pl.ANY),
            pl.BlockSpec(memory_space=pltpu.VMEM),
            pl.BlockSpec(memory_space=pl.ANY),
        ],
        out_specs=pl.BlockSpec(memory_space=pltpu.VMEM),
        scratch_shapes=scratch,
        compiler_params=pltpu.CompilerParams(
            collective_id=0, has_side_effects=True, vmem_limit_bytes=(20 if n <= 8 else 58) * 2**20
        ),
        cost_estimate=pl.CostEstimate(flops=flops, bytes_accessed=orbitals.size * 2, transcendentals=0),
    )(orbitals, points.reshape(1, pts), kernel.reshape(row_total, n, pts))


def solution(mesh):
    in_specs = (
        P(("group", "prow", "pcol"), None),
        P(("group", "prow", "pcol")),
        P(("group", "prow"), None, "pcol", None),
    )
    out_specs = P(("group", "prow"), "pcol")
    return jax.shard_map(
        functools.partial(shards, mesh.shape["prow"]),
        mesh=mesh, in_specs=in_specs, out_specs=out_specs, check_vma=False,
    )
```

time: 82.9 us -> 31.9 us (0.38)
  waiting for transfers between devices: 54.1 us -> 0 us
  Pallas kernels: 0 us -> 27.7 us
  between operations: 13.4 us -> 0.01 us
  other arithmetic: 5.2 us -> 0 us
  matrix products: 4.77 us -> 0 us
  blocking collectives: 3.82 us -> 0 us
  local copies, waits for them, and re-layouts: 0.99 us -> 3.99 us
    all_gather x1 -> x0, waiting for transfers between devices: 45.4 us -> none  [shards(): column_values = lax.all_gather(sampled, 'prow', axis=0, tiled=True)]
    pallas_call x0 -> x1, Pallas kernels: none -> 27.7 us  [shards(): pl.pallas_call(functools.partial(body, n), out_shape=jax.ShapeDtypeStruct...]
    reduce_scatter x1 -> x0, waiting for transfers between devices: 8.66 us -> none  [shards(): lax.psum_scatter(partial_sum, 'pcol', scatter_dimension=1, tiled=True)]
    dot_general x1 -> x0, matrix products: 4.77 us -> none  [shards(): jnp.dot(screened, column_values, preferred_element_type=jnp.float32)]
    unnamed x2 -> x7, local copies, waits for them, and re-layouts: 0.13 us -> 3.99 us
    all_gather x1 -> x0, blocking collectives: 3.82 us -> none  [shards(): own_rows = lax.all_gather(sampled, 'pcol', axis=0, tiled=True)]
    convert_element_type x1 -> x0, other arithmetic: 1.77 us -> none  [shards(): lax.psum_scatter(partial_sum, 'pcol', scatter_dimension=1, tiled=True)]
    select_n x2 -> x0, other arithmetic: 1.45 us -> none  [shards(): sampled = jnp.take(orbitals, points, axis=0)]
  transfers between devices with their start and end apart: 2 -> 0, of which waited for: 2 -> 0; matrix products, arithmetic and copies ran while one was open for 1% -> 0% of each run, Pallas kernels for 0% -> 0%
where the time goes in v1:
time: 31.9 us; the launch traced here: 31.7 us
  Pallas kernels  27.7 us (87%)
  local copies, waits for them, and re-layouts  3.99 us (13%)
    pallas_call x1, Pallas kernels, shards(): pl.pallas_call(functools.partial(body, n), out_shape=jax.ShapeDtypeStruct...  27.7 us
    unnamed x7, local copies, waits for them, and re-layouts  3.99 us

profile of v1, /device:TPU:1, one launch (start us, length us, event | category | flops | bytes accessed | tf_op | source)
XLA Modules:
  0.0 31.7 jit_solution(18403742939595661109)
XLA Ops:
  0.0 0.0 copy-start
  0.0 1.6 %copy-done = bf16[1024,1024]{1,0:T(8,128)(2,1)S(1)} copy-done((bf16[1024,1024]{1,0:T(8,128)(2,1)S(1)}, bf16[1024,1024]{1,0:T(8,128)(2,1)}, u32[]{:S(2)}) %copy-start) | copy-done | bytes 2097176
  1.6 0.0 copy-start.1
  1.6 1.0 %copy-done.1 = bf16[256,8,1,128]{3,1,2,0:T(8,128)(2,1)S(1)} copy-done((bf16[256,8,1,128]{3,1,2,0:T(8,128)(2,1)S(1)}, bf16[256,8,1,128]{3,1,2,0:T(8,128)(2,1)}, u32[]{:S(2)}) %copy-start.1) | copy-done | bytes 524312
  2.6 0.0 copy-start.2
  2.6 0.7 %copy-done.2 = s32[128]{0:T(128)S(1)} copy-done((s32[128]{0:T(128)S(1)}, s32[128]{0:T(128)}, u32[]{:S(2)}) %copy-start.2) | copy-done | bytes 536
  3.3 27.7 %shard_map.37 = bf16[256,512]{1,0:T(8,128)(2,1)S(1)} custom-call(bf16[1024,1024]{1,0:T(8,128)(2,1)S(1)} %copy-done, s32[1,128]{1,0:T(1,128)S(1)} %bitcast.3, bf16[256,8,128]{2,1,0:T(8,128)(2,1)S(1)} %bitcast.2), custom_call_target="tpu_custom_call" | custom-call | flops 1073741824 | bytes 2097152 | tf_op jit(solution)/shard_map/pallas_call | solution.py:252
  31.0 0.7 %copy.5 = bf16[256,512]{1,0:T(8,128)(2,1)} copy(bf16[256,512]{1,0:T(8,128)(2,1)S(1)} %shard_map.37) | data formatting | bytes 524288
Async XLA Ops:
  0.0 1.6 %copy-start = (bf16[1024,1024]{1,0:T(8,128)(2,1)S(1)}, bf16[1024,1024]{1,0:T(8,128)(2,1)}, u32[]{:S(2)}) copy-start(bf16[1024,1024]{1,0:T(8,128)(2,1)} %orb_hbm.1) | copy-start | bytes 6291460
  1.6 1.0 %copy-start.1 = (bf16[256,8,1,128]{3,1,2,0:T(8,128)(2,1)S(1)}, bf16[256,8,1,128]{3,1,2,0:T(8,128)(2,1)}, u32[]{:S(2)}) copy-start(bf16[256,8,1,128]{3,1,2,0:T(8,128)(2,1)} %param.5) | copy-start | bytes 1572868
  2.6 0.7 %copy-start.2 = (s32[128]{0:T(128)S(1)}, s32[128]{0:T(128)}, u32[]{:S(2)}) copy-start(s32[128]{0:T(128)} %param.4) | copy-start | bytes 1540

commit v2 on v1

--- a/solution.py
+++ b/solution.py
@@ -25,9 +25,9 @@
 
 
 def body(
-    n, orb_hbm, pts_ref, ker_hbm, out_ref,
-    orb, ker, ker32, rows, blocks, sib_blocks, scr, sib_scr, acc,
-    orb_sem, ker_sem, row_send, row_recv, ring_send, ring_recv, blk_send, blk_recv, scr_send, scr_recv,
+    n, orb_hbm, pts_hbm, ker_hbm, out_ref,
+    pts_ref, orb, ker, ker32, rows, blocks, sib_blocks, scr, sib_scr, acc,
+    pts_sem, orb_sem, ker_sem, row_send, row_recv, ring_send, ring_recv, blk_send, blk_recv, scr_send, scr_recv,
 ):
     last = n // 2
     pts = pts_ref.shape[1]
@@ -83,6 +83,8 @@
     loads = [
         pltpu.make_async_copy(orb_hbm.at[:, pl.ds(c * wide, wide)], orb.at[c], orb_sem.at[c]) for c in range(CH)
     ]
+    pts_load = pltpu.make_async_copy(pts_hbm, pts_ref, pts_sem)
+    pts_load.start()
     for c in order:
         loads[c].start()
     ker_load = pltpu.make_async_copy(ker_hbm, ker, ker_sem)
@@ -92,6 +94,7 @@
     for device in (left, right, sibling):
         pl.semaphore_signal(barrier, inc=1, device_id=device, device_id_type=MESH)
 
+    pts_load.wait()
     wanted = jnp.transpose(jnp.broadcast_to(pts_ref[...], (pts, pts)))
     wanted = jnp.concatenate([wanted] * (grid_rows // pts), axis=1)
     hot = (wanted == lax.broadcasted_iota(jnp.int32, (pts, grid_rows), 1)).astype(jnp.float32).astype(jnp.bfloat16)
@@ -228,6 +231,7 @@
     bf16, f32 = jnp.bfloat16, jnp.float32
     dma = pltpu.SemaphoreType.DMA
     scratch = [
+        pltpu.VMEM((1, pts), jnp.int32),
         pltpu.VMEM((CH, grid_rows, wide), bf16),
         pltpu.VMEM((row_total, n, pts), bf16),
         pltpu.VMEM((row_total * n, pts), f32),
@@ -237,6 +241,7 @@
         pltpu.VMEM((slots, row_total, 2 * pts), bf16),
         pltpu.VMEM((slots, row_total, 2 * pts), bf16),
         pltpu.VMEM((HALF, row_total, wide), f32),
+        dma,
         dma((CH,)),
         dma,
         dma((CH,)),
@@ -251,16 +256,16 @@
     flops = 4 * row_total * n * pts * nocc
     return pl.pallas_call(
         functools.partial(body, n),
-        out_shape=jax.ShapeDtypeStruct((row_total, nocc // 2), bf16),
+        out_shape=pltpu.VMEM((row_total, nocc // 2), bf16),
         in_specs=[
             pl.BlockSpec(memory_space=pl.ANY),
-            pl.BlockSpec(memory_space=pltpu.VMEM),
+            pl.BlockSpec(memory_space=pl.ANY),
             pl.BlockSpec(memory_space=pl.ANY),
         ],
         out_specs=pl.BlockSpec(memory_space=pltpu.VMEM),
         scratch_shapes=scratch,
         compiler_params=pltpu.CompilerParams(
-            collective_id=0, has_side_effects=True, vmem_limit_bytes=(20 if n <= 8 else 58) * 2**20
+            collective_id=0, has_side_effects=True, vmem_limit_bytes=60 * 2**20
         ),
         cost_estimate=pl.CostEstimate(flops=flops, bytes_accessed=orbitals.size * 2, transcendentals=0),
     )(orbitals, points.reshape(1, pts), kernel.reshape(row_total, n, pts))

time: 31.9 us -> 28.5 us (0.89)
  local copies, waits for them, and re-layouts: 3.99 us -> 0.71 us
    unnamed x7 -> x1, local copies, waits for them, and re-layouts: 3.99 us -> 0.71 us
where the time goes in v2:
time: 28.5 us; the launch traced here: 28.4 us
  Pallas kernels  27.6 us (97%)
  local copies, waits for them, and re-layouts  0.71 us (2%)
    pallas_call x1, Pallas kernels, shards(): pl.pallas_call(functools.partial(body, n), out_shape=pltpu.VMEM((row_tota...  27.6 us
    unnamed x1, local copies, waits for them, and re-layouts  0.71 us

profile of v2, /device:TPU:1, one launch (start us, length us, event | category | flops | bytes accessed | tf_op | source)
XLA Modules:
  0.0 28.4 jit_solution(15057616367216240940)
XLA Ops:
  0.0 27.6 %shard_map.37 = bf16[256,512]{1,0:T(8,128)(2,1)S(1)} custom-call(bf16[1024,1024]{1,0:T(8,128)(2,1)} %orb_hbm.1, s32[1,128]{1,0:T(1,128)} %bitcast.3, bf16[256,8,128]{2,1,0:T(8,128)(2,1)} %bitcast.2), custom_call_target="tpu_custom_call" | custom-call | flops 1073741824 | bytes 2097152 | tf_op jit(solution)/shard_map/pallas_call | solution.py:257
  27.7 0.7 %copy.5 = bf16[256,512]{1,0:T(8,128)(2,1)} copy(bf16[256,512]{1,0:T(8,128)(2,1)S(1)} %shard_map.37) | data formatting | bytes 524288

commit v3 on v2

--- a/solution.py
+++ b/solution.py
@@ -111,7 +111,7 @@
         hop(1, 0, c).start()
 
     ker_load.wait()
-    ker32[...] = ker[...].astype(jnp.float32).reshape(ker32.shape)
+    ker32[pl.ds(0, ker.shape[0] * n), :] = ker[...].astype(jnp.float32).reshape(ker.shape[0] * n, pts)
 
     for c in range(CH):
         row_arrival(c).wait_recv()
@@ -234,7 +234,7 @@
         pltpu.VMEM((1, pts), jnp.int32),
         pltpu.VMEM((CH, grid_rows, wide), bf16),
         pltpu.VMEM((row_total, n, pts), bf16),
-        pltpu.VMEM((row_total * n, pts), f32),
+        pltpu.VMEM(((row_total + 1) * n, pts), f32),
         pltpu.VMEM((CH, row_total, wide), bf16),
         pltpu.VMEM((slots, CH, 2 * pts, wide), bf16),
         pltpu.VMEM((slots, HALF, 2 * pts, wide), bf16),

time: 28.5 us -> 28.5 us (level)
  no operation moved by 1% of the time
where the time goes in v3:
time: 28.5 us; the launch traced here: 28.4 us
  Pallas kernels  27.6 us (97%)
  local copies, waits for them, and re-layouts  0.71 us (2%)
    pallas_call x1, Pallas kernels, shards(): pl.pallas_call(functools.partial(body, n), out_shape=pltpu.VMEM((row_tota...  27.6 us
    unnamed x1, local copies, waits for them, and re-layouts  0.71 us

profile of v3, /device:TPU:1, one launch (start us, length us, event | category | flops | bytes accessed | tf_op | source)
XLA Modules:
  0.0 28.4 jit_solution(14848852922440162597)
XLA Ops:
  0.0 27.6 %shard_map.37 = bf16[256,512]{1,0:T(8,128)(2,1)S(1)} custom-call(bf16[1024,1024]{1,0:T(8,128)(2,1)} %orb_hbm.1, s32[1,128]{1,0:T(1,128)} %bitcast.3, bf16[256,8,128]{2,1,0:T(8,128)(2,1)} %bitcast.2), custom_call_target="tpu_custom_call" | custom-call | flops 1073741824 | bytes 2097152 | tf_op jit(solution)/shard_map/pallas_call | solution.py:257
  27.7 0.7 %copy.5 = bf16[256,512]{1,0:T(8,128)(2,1)} copy(bf16[256,512]{1,0:T(8,128)(2,1)S(1)} %shard_map.37) | data formatting | bytes 524288

commit v4 on v3

--- a/solution.py
+++ b/solution.py
@@ -25,8 +25,8 @@
 
 
 def body(
-    n, orb_hbm, pts_hbm, ker_hbm, out_ref,
-    pts_ref, orb, ker, ker32, rows, blocks, sib_blocks, scr, sib_scr, acc,
+    n, orb_hbm, pts_hbm, ker_hbm, out_ref, both_ref, vals_ref,
+    pts_ref, orb, ker, ker32, rows, blocks, sib_blocks, scr, sib_scr,
     pts_sem, orb_sem, ker_sem, row_send, row_recv, ring_send, ring_recv, blk_send, blk_recv, scr_send, scr_recv,
 ):
     last = n // 2
@@ -69,6 +69,16 @@
             )
         return remote(blocks.at[s, far], sib_blocks.at[s], blk_send.at[s], blk_recv.at[s], sibling)
 
+    def last_copy(i):
+        return remote(
+            blocks.at[last, (1 - core) * HALF + i, side[0]], vals_ref.at[pl.ds(pts, pts), pl.ds(i * wide, wide)],
+            blk_send.at[last - last * i], blk_recv.at[last - last * i], sibling,
+        )
+
+    last_scr = remote(
+        scr.at[last, :, side[0]], both_ref.at[:, pl.ds(pts, pts)], scr_send.at[last], scr_recv.at[last], sibling
+    )
+
     def scr_copy(s, narrow=False):
         if narrow:
             return remote(
@@ -122,18 +132,18 @@
     scr[0, :, side[0]] = screened
     scr_copy(0, True).start()
     for i in range(HALF):
-        acc[i] = dot(screened, rows[core * HALF + i, mine])
+        out_ref[:, pl.ds(i * wide, wide)] = dot(screened, rows[core * HALF + i, mine])
 
     def late(s):
         scr_copy(s).wait_recv()
         blk_copy(s).wait_recv()
         for i in range(HALF):
-            acc[i] += dot(sib_scr[s], sib_blocks[s, i])
+            out_ref[:, pl.ds(i * wide, wide)] += dot(sib_scr[s], sib_blocks[s, i])
 
     def late_first():
         scr_copy(0, True).wait_recv()
         for i in range(HALF):
-            acc[i] += dot(sib_scr[0, :, side[0]], rows[core * HALF + i, theirs])
+            out_ref[:, pl.ds(i * wide, wide)] += dot(sib_scr[0, :, side[0]], rows[core * HALF + i, theirs])
 
     def step(s):
         for k in range(CH):
@@ -152,7 +162,7 @@
         scr[s] = screened
         scr_copy(s).start()
         for i in range(HALF):
-            acc[i] += dot(screened, blocks[s, core * HALF + i])
+            out_ref[:, pl.ds(i * wide, wide)] += dot(screened, blocks[s, core * HALF + i])
 
     step(1)
     late_first()
@@ -169,6 +179,27 @@
 
     step(last - 1)
     late(last - 2)
+
+    def drain(s):
+        for c in range(CH):
+            for way in (0, 1):
+                hop(way, s, c).wait_send()
+
+    def drain_pair(s):
+        scr_copy(s).wait_send()
+        blk_copy(s).wait_send()
+
+    for c in range(CH):
+        row_copy(c).wait_send()
+    drain(0)
+    drain(1)
+    scr_copy(0, True).wait_send()
+    if last == 4:
+        drain_pair(1)
+        drain_pair(2)
+    else:
+        pl.loop(2, last - 2)(drain)
+        pl.loop(1, last - 1)(drain_pair)
 
     far = side[0]
     for k in range(HALF):
@@ -176,50 +207,23 @@
         hop(1, last - 1, k + HALF).wait_recv()
         part = dot_t(rows[k], blocks[last, k, far]) + dot_t(rows[k + HALF], blocks[last, k + HALF, far])
         density = part if k == 0 else density + part
-    blk_copy(last, True).start()
+    for i in range(HALF):
+        last_copy(i).start()
     screened = (kernel_columns(ring_index((pos + last) % n, n)) * density).astype(jnp.bfloat16)
     scr[last, :, far] = screened
-    scr_copy(last, True).start()
+    last_scr.start()
     late(last - 1)
-    for i in range(HALF):
-        acc[i] += dot(screened, blocks[last, core * HALF + i, far])
-    blk_copy(last, True).wait_recv()
-    scr_copy(last, True).wait_recv()
-    for i in range(HALF):
-        total = acc[i] + dot(sib_scr[last, :, far], sib_blocks[last, i, far])
-        out_ref[:, pl.ds(i * wide, wide)] = total.astype(out_ref.dtype)
-
-    for c in range(CH):
-        row_copy(c).wait_send()
-        for way in (0, 1):
-            hop(way, 0, c).wait_send()
-            hop(way, 1, c).wait_send()
-
-    def drain(s):
-        for c in range(CH):
-            for way in (0, 1):
-                hop(way, s, c).wait_send()
-
-    if last == 4:
-        drain(2)
-    else:
-        pl.loop(2, last - 1)(drain)
+    both_ref[:, pl.ds(0, pts)] = screened
+    for i in range(HALF):
+        vals_ref[pl.ds(0, pts), pl.ds(i * wide, wide)] = blocks[last, core * HALF + i, far]
+    drain(last - 2)
     for k in range(HALF):
         hop(0, last - 1, k).wait_send()
         hop(1, last - 1, k + HALF).wait_send()
-    scr_copy(0, True).wait_send()
-    scr_copy(last, True).wait_send()
-    blk_copy(last, True).wait_send()
-
-    def drain_pair(s):
-        scr_copy(s).wait_send()
-        blk_copy(s).wait_send()
-
-    if last == 4:
-        for s in range(1, last):
-            drain_pair(s)
-    else:
-        pl.loop(1, last)(drain_pair)
+    drain_pair(last - 1)
+    for i in range(HALF):
+        last_copy(i).wait()
+    last_scr.wait()
 
 
 def shards(n, orbitals, points, kernel):
@@ -240,7 +244,6 @@
         pltpu.VMEM((slots, HALF, 2 * pts, wide), bf16),
         pltpu.VMEM((slots, row_total, 2 * pts), bf16),
         pltpu.VMEM((slots, row_total, 2 * pts), bf16),
-        pltpu.VMEM((HALF, row_total, wide), f32),
         dma,
         dma((CH,)),
         dma,
@@ -254,21 +257,26 @@
         dma((slots,)),
     ]
     flops = 4 * row_total * n * pts * nocc
-    return pl.pallas_call(
+    total, screened, values = pl.pallas_call(
         functools.partial(body, n),
-        out_shape=pltpu.VMEM((row_total, nocc // 2), bf16),
+        out_shape=(
+            pltpu.VMEM((row_total, nocc // 2), f32),
+            pltpu.VMEM((row_total, 2 * pts), bf16),
+            pltpu.VMEM((2 * pts, nocc // 2), bf16),
+        ),
         in_specs=[
             pl.BlockSpec(memory_space=pl.ANY),
             pl.BlockSpec(memory_space=pl.ANY),
             pl.BlockSpec(memory_space=pl.ANY),
         ],
-        out_specs=pl.BlockSpec(memory_space=pltpu.VMEM),
+        out_specs=(pl.BlockSpec(memory_space=pltpu.VMEM),) * 3,
         scratch_shapes=scratch,
         compiler_params=pltpu.CompilerParams(
             collective_id=0, has_side_effects=True, vmem_limit_bytes=60 * 2**20
         ),
         cost_estimate=pl.CostEstimate(flops=flops, bytes_accessed=orbitals.size * 2, transcendentals=0),
     )(orbitals, points.reshape(1, pts), kernel.reshape(row_total, n, pts))
+    return (total + dot(screened, values)).astype(bf16)
 
 
 def solution(mesh):

time: 28.5 us -> 28.5 us (level)
  matrix products: 0 us -> 0.93 us
  local copies, waits for them, and re-layouts: 0.71 us -> 0 us
  Pallas kernels: 27.6 us -> 27.3 us
    dot_general x0 -> x1, matrix products: none -> 0.93 us  [dot(): return jnp.dot(a, b, preferred_element_type=jnp.float32)]
    unnamed x1 -> x0, local copies, waits for them, and re-layouts: 0.71 us -> none
    pallas_call x1, Pallas kernels: 27.6 us -> 27.3 us  [shards(): pl.pallas_call(functools.partial(body, n), out_shape=(pltpu.VMEM((row_tot...]
where the time goes in v4:
time: 28.5 us; the launch traced here: 28.3 us
  Pallas kernels  27.3 us (96%)
  matrix products  0.93 us (3%)
    pallas_call x1, Pallas kernels, shards(): pl.pallas_call(functools.partial(body, n), out_shape=(pltpu.VMEM((row_tot...  27.3 us
    dot_general x1, matrix products, dot(): return jnp.dot(a, b, preferred_element_type=jnp.float32)  0.93 us

profile of v4, /device:TPU:1, one launch (start us, length us, event | category | flops | bytes accessed | tf_op | source)
XLA Modules:
  0.0 28.3 jit_solution(5314921904487492379)
XLA Ops:
  0.0 27.3 %shard_map.37 = (f32[256,512]{1,0:T(8,128)S(1)}, bf16[256,256]{1,0:T(8,128)(2,1)S(1)}, bf16[256,512]{1,0:T(8,128)(2,1)S(1)}) custom-call(bf16[1024,1024]{1,0:T(8,128)(2,1)} %orb_hbm.1, s32[1,128]{1,0:T(1,128)} %bitcast.5, bf16[256,8,128]{2,1,0:T(8,128)(2,1)} %bitcast.4), custom_call_target="tpu_custom_call" | custom-call | flops 1073741824 | bytes 2097152 | tf_op jit(solution)/shard_map/pallas_call | solution.py:260
  27.3 0.9 %fusion = bf16[256,512]{1,0:T(8,128)(2,1)} fusion(f32[256,512]{1,0:T(8,128)S(1)} %get-tuple-element.8, bf16[256,256]{1,0:T(8,128)(2,1)S(1)} %get-tuple-element.9, bf16[256,512]{1,0:T(8,128)(2,1)S(1)} %get-tuple-element.10), kind=kOutput, calls=%fused_computation.1 | convolution fusion | flops 67371008 | bytes 1179648 | tf_op jit(solution)/shard_map/dot_general | solution.py:20

commit v5 on v3

--- a/solution.py
+++ b/solution.py
@@ -85,10 +85,10 @@
     ]
     pts_load = pltpu.make_async_copy(pts_hbm, pts_ref, pts_sem)
     pts_load.start()
-    for c in order:
-        loads[c].start()
+    for k, c in enumerate(order):
+        loads[c].start(priority=1 if k else 0)
     ker_load = pltpu.make_async_copy(ker_hbm, ker, ker_sem)
-    ker_load.start()
+    ker_load.start(priority=1)
 
     barrier = pltpu.get_barrier_semaphore()
     for device in (left, right, sibling):

time: 28.5 us -> 28.3 us (level)
  no operation moved by 1% of the time
where the time goes in v5:
time: 28.3 us; the launch traced here: 28.1 us
  Pallas kernels  27.4 us (97%)
  local copies, waits for them, and re-layouts  0.71 us (3%)
    pallas_call x1, Pallas kernels, shards(): pl.pallas_call(functools.partial(body, n), out_shape=pltpu.VMEM((row_tota...  27.4 us
    unnamed x1, local copies, waits for them, and re-layouts  0.71 us

profile of v5, /device:TPU:1, one launch (start us, length us, event | category | flops | bytes accessed | tf_op | source)
XLA Modules:
  0.0 28.1 jit_solution(17532347445925029711)
XLA Ops:
  0.0 27.4 %shard_map.37 = bf16[256,512]{1,0:T(8,128)(2,1)S(1)} custom-call(bf16[1024,1024]{1,0:T(8,128)(2,1)} %orb_hbm.1, s32[1,128]{1,0:T(1,128)} %bitcast.3, bf16[256,8,128]{2,1,0:T(8,128)(2,1)} %bitcast.2), custom_call_target="tpu_custom_call" | custom-call | flops 1073741824 | bytes 2097152 | tf_op jit(solution)/shard_map/pallas_call | solution.py:257
  27.4 0.7 %copy.5 = bf16[256,512]{1,0:T(8,128)(2,1)} copy(bf16[256,512]{1,0:T(8,128)(2,1)S(1)} %shard_map.37) | data formatting | bytes 524288

commit v6 on v5

--- a/solution.py
+++ b/solution.py
@@ -86,7 +86,7 @@
     pts_load = pltpu.make_async_copy(pts_hbm, pts_ref, pts_sem)
     pts_load.start()
     for k, c in enumerate(order):
-        loads[c].start(priority=1 if k else 0)
+        loads[c].start(priority=1 if k > 1 else 0)
     ker_load = pltpu.make_async_copy(ker_hbm, ker, ker_sem)
     ker_load.start(priority=1)
 

time: 28.3 us -> 28.3 us (level)
  no operation moved by 1% of the time
where the time goes in v6:
time: 28.3 us; the launch traced here: 28.2 us
  Pallas kernels  27.5 us (97%)
  local copies, waits for them, and re-layouts  0.71 us (3%)
    pallas_call x1, Pallas kernels, shards(): pl.pallas_call(functools.partial(body, n), out_shape=pltpu.VMEM((row_tota...  27.5 us
    unnamed x1, local copies, waits for them, and re-layouts  0.71 us

profile of v6, /device:TPU:1, one launch (start us, length us, event | category | flops | bytes accessed | tf_op | source)
XLA Modules:
  0.0 28.2 jit_solution(12881982827786331143)
XLA Ops:
  0.0 27.5 %shard_map.37 = bf16[256,512]{1,0:T(8,128)(2,1)S(1)} custom-call(bf16[1024,1024]{1,0:T(8,128)(2,1)} %orb_hbm.1, s32[1,128]{1,0:T(1,128)} %bitcast.3, bf16[256,8,128]{2,1,0:T(8,128)(2,1)} %bitcast.2), custom_call_target="tpu_custom_call" | custom-call | flops 1073741824 | bytes 2097152 | tf_op jit(solution)/shard_map/pallas_call | solution.py:257
  27.5 0.7 %copy.5 = bf16[256,512]{1,0:T(8,128)(2,1)} copy(bf16[256,512]{1,0:T(8,128)(2,1)S(1)} %shard_map.37) | data formatting | bytes 524288
